TPU v7x, 128 devices: a whole 4x4x4 slice. The times are simulated.
128 devices in a mesh: block: 32 (over z, y, x_hi), slab: 2 (over core), event: 2 (over x_lo).
Axes of the slice: x: 4 (x_hi: 2, x_lo: 2; x = x_hi * 2 + x_lo), y: 4, z: 4, core: 2. Of those that a mesh axis runs over, the one named last changes fastest.
Arguments:
- adjoint_start: float32 [4, 1024, 32, 512], P('event', 'block', 'slab'), may hold values from -3 to 3
- velocity_start: float32 [4, 1024, 32, 512], P('event', 'block', 'slab'), may hold values from -3 to 3
- source_field: float32 [4, 1024, 32, 512], P('event', 'block', 'slab'), may hold values from -6 to 6
- source_time: float32 [4, 4], P('event'), may hold values from -4 to 4
- modulus: float32 [1024, 32, 512], P('block', 'slab'), may hold values from 1 to 4
- inverse_mass: float32 [1024, 32, 512], P('block', 'slab'), may hold values from 1 to 3
- crust_depth: int32 [1024, 512], P('block'), may hold values from 1 to 8
Outputs:
- adjoint_end: float32 [4, 1024, 32, 512], P('event', 'block', 'slab')
- hessian: float32 [1024, 32, 512], P('block', 'slab')
All inputs are finite; a program needn't handle non-finite values.
Results may differ from a plain program's by a relative error of at most 0.0001.
Values sent between devices are 32-bit elements; how exact they have to be, the bound alone decides.
A program may use at most 128 MiB of HBM per device.

v0:
```python
import functools

import jax
import jax.numpy as jnp
import numpy as np
from jax import lax
from jax.experimental import pallas as pl
from jax.experimental.pallas import tpu as pltpu
from jax.sharding import PartitionSpec as P

STEPS = 4
TIME_STEP = 0.1
CRUST_FACTOR = 0.35
WEIGHTS = (0.1, 49.0 / 90.0, 32.0 / 45.0, 49.0 / 90.0, 0.1)
ASSEMBLED = (0.2, 49.0 / 90.0, 32.0 / 45.0, 49.0 / 90.0)
MESH = pl.DeviceIdType.MESH
TILE = (8, 128)


def derivative_table():
    points = np.array([-1.0, -np.sqrt(3.0 / 7.0), 0.0, np.sqrt(3.0 / 7.0), 1.0])
    scales = np.array(
        [
            np.prod([points[one] - points[other] for other in range(5) if other != one])
            for one in range(5)
        ]
    )
    table = np.zeros((5, 5))
    for target in range(5):
        for anchor in range(5):
            if target != anchor:
                table[target, anchor] = scales[target] / (
                    scales[anchor] * (points[target] - points[anchor])
                )
        table[target, target] = -np.sum(table[target])
    return table


D = derivative_table()
A4, B4 = (D[4, 4] - D[4, 0]) / 2, (D[4, 3] - D[4, 1]) / 2
E4, T4 = (D[4, 4] + D[4, 0]) / 2, (D[4, 3] + D[4, 1]) / 2
A3, B3 = (D[3, 4] - D[3, 0]) / 2, (D[3, 3] - D[3, 1]) / 2
E3, T3 = (D[3, 4] + D[3, 0]) / 2, (D[3, 3] + D[3, 1]) / 2
SCALE = (A4, A3, D[2, 3], A3, A4)
DN = D / np.array(SCALE)[:, None]
KAPPA0, GAMMA, DELTA = B4 / A4, E4 / A4, T4 / A4
KAPPA1, EPSILON, ZETA = B3 / A3, E3 / A3, T3 / A3
KAPPA2 = D[2, 4] / D[2, 3]
RHO = [WEIGHTS[i] * SCALE[i] ** 2 for i in range(5)]


def line(u0, u1, u2, u3, u4, c0, c1, c2, c3, c4, last=True):
    a, b = u4 - u0, u3 - u1
    twice = u2 + u2
    e, f = (u4 + u0) - twice, (u3 + u1) - twice
    p, q = a + KAPPA0 * b, GAMMA * e + DELTA * f
    r, s = a + KAPPA1 * b, EPSILON * e + ZETA * f
    h4, h0 = (p + q) * c4, (p - q) * c0
    h3, h1 = (r + s) * c3, (r - s) * c1
    h2 = (b + KAPPA2 * a) * c2
    hp, hm = h4 + h0, h4 - h0
    ep, em = h3 + h1, h3 - h1
    fa = (hp + ep) + KAPPA2 * h2
    fb = (KAPPA0 * hp + KAPPA1 * ep) + h2
    fe = GAMMA * hm + EPSILON * em
    ff = DELTA * hm + ZETA * em
    total = fe + ff
    return fe - fa, ff - fb, total + total, ff + fb, (fe + fa if last else None)


def body(slabs, blocks, *refs):
    (
        start_hbm, velocity_hbm, source_hbm, time_ref, modulus_hbm, mass_hbm, crust_hbm,
        end_ref, hessian_ref,
        nat_u, nat_v, nat_s, nat_g, nat_m, nat_c,
        u, w, sf, im, hs, gx, gy, gz, uy, gy4, gz4, kx, kdx, kz, kdz, ub, pb, fs, fy,
        zs, zh, gzs, gzh, layer, crust, sent, got, index,
        in_sem, end_sem, zsend, zrecv, gzsend, gzrecv, gsend, grecv,
        usend, urecv, psend, precv, qsend, qrecv, hsend, hrecv,
    ) = refs
    block = lax.axis_index("block")
    slab = lax.axis_index("slab")
    event = lax.axis_index("event")
    before = (lax.rem(block + blocks - 1, blocks), slab, event)
    after = (lax.rem(block + 1, blocks), slab, event)
    other_slab = (block, 1 - slab, event)
    other_event = (block, slab, 1 - event)

    barrier = pltpu.get_barrier_semaphore()
    for device in (before, after, other_slab, other_event):
        pl.semaphore_signal(barrier, inc=1, device_id=device, device_id_type=MESH)

    def start_loads(j):
        at = pl.ds(4 * j, 4)
        for k in range(4):
            lanes = (slice(None), pl.ds(128 * k, 128))
            pairs = [(modulus_hbm.at[at, *lanes], nat_g.at[k, at], 0)]
            for e in range(2):
                pairs.append((start_hbm.at[e, at, *lanes], nat_u.at[k, at, e], 1))
            pairs.append((mass_hbm.at[at, *lanes], nat_m.at[k, at], 2))
            for e in range(2):
                pairs.append((source_hbm.at[e, at, *lanes], nat_s.at[k, at, e], 3))
                pairs.append((velocity_hbm.at[e, at, *lanes], nat_v.at[k, at, e], 4))
            for source, target, kind in pairs:
                pltpu.make_async_copy(source, target, in_sem.at[j, kind]).start()

    def wait_load(ref, j, kind):
        whole = ref.at[:, pl.ds(4 * j, 4)]
        pltpu.make_async_copy(whole, whole, in_sem.at[j, kind]).wait()

    crust_load = pltpu.make_async_copy(crust_hbm, nat_c, gsend)
    crust_load.start()

    @pl.loop(0, 8)
    def _(n):
        start_loads(lax.rem(7 * n, 8))

    lane = lax.broadcasted_iota(jnp.int32, TILE, 1)
    row = lax.broadcasted_iota(jnp.int32, TILE, 0)
    radial = row & 3
    for r in range(4):
        index[r] = 4 * (lane & 31) + ((r - (lane >> 5)) & 3)
        index[4 + r] = 32 * ((r - (lane & 3)) & 3) + (lane >> 2)
    bit0, bit1 = (lane & 1) == 1, (lane & 2) == 2
    block0, block1 = (lane & 32) == 32, (lane & 64) == 64
    upper = row < 4
    is0 = jnp.where(slab == 0, 1.0, 0.0).astype(jnp.float32)
    is1 = 1.0 - is0

    def gather(value, k):
        return jnp.take_along_axis(value, index[k], axis=1)

    def apart(t):
        x = [jnp.where(bit0, t[(r + 3) % 4], t[r]) for r in range(4)]
        m = [jnp.where(bit1, x[(r + 2) % 4], x[r]) for r in range(4)]
        n = [gather(m[r], r) for r in range(4)]
        y = [jnp.where(block0, n[(k + 1) % 4], n[k]) for k in range(4)]
        return [jnp.where(block1, y[(k + 2) % 4], y[k]) for k in range(4)]

    def together(o):
        y = [jnp.where(block0, o[(r + 3) % 4], o[r]) for r in range(4)]
        n = [jnp.where(block1, y[(r + 2) % 4], y[r]) for r in range(4)]
        m = [gather(n[r], 4 + r) for r in range(4)]
        z = [jnp.where(bit0, m[(k + 1) % 4], m[k]) for k in range(4)]
        return [jnp.where(bit1, z[(k + 2) % 4], z[k]) for k in range(4)]

    def turn(value, shift):
        return value if shift % 8 == 0 else pltpu.roll(value, shift % 8, 0)

    def pack(values, at):
        result = turn(values[0], -at)
        for k in range(1, 4):
            result = jnp.where(radial == k, turn(values[k], k - at), result)
        return result

    def next_lane(value):
        return jnp.where(lane == 127, 0.0, pltpu.roll(value, 127, 1))

    def lane_before(value):
        return jnp.where(lane == 0, 0.0, pltpu.roll(value, 1, 1))

    def twice_events(value):
        other = pltpu.roll(value, 4, 0)
        return jnp.where(upper, value, other), jnp.where(upper, other, value)

    def rows_of(ref, per):
        return ref.reshape(4 * 32 * per, 128)

    rows_u, rows_v, rows_s = rows_of(nat_u, 32), rows_of(nat_v, 32), rows_of(nat_s, 32)
    rows_g, rows_m, rows_sent = rows_of(nat_g, 16), rows_of(nat_m, 16), rows_of(sent, 16)

    def strided(ref, first, count):
        return [ref[pl.ds(first + count * k, 8, stride=4), :] for k in range(4)]

    edge_z = jnp.where(slab == 0, jnp.where(radial == 0, 0.1, 0.2), 0.2).astype(jnp.float32)
    edge_y = jnp.where(lane == 0, 0.1, 0.2).astype(jnp.float32)

    def over_z(value, zm):
        return value * (edge_z if zm == 0 else ASSEMBLED[zm])

    def over_y(value, ym):
        return value * (edge_y if ym == 0 else ASSEMBLED[ym])

    crust_load.wait()

    @pl.loop(0, 4)
    def _(part):
        at = pl.ds(pl.multiple_of(8 * part, 8), 8)
        found = apart([nat_c[at, pl.ds(128 * k, 128)] for k in range(4)])
        for k in range(4):
            crust[k, at, :] = found[k]

    def set_up(j):
        wait_load(nat_g, j, 0)
        gxj, gyj, gzj = gx.at[j], gy.at[j], gz.at[j]
        for half in range(2):
            x = 4 * j + 2 * half
            depth = [
                jnp.where(
                    upper,
                    jnp.broadcast_to(crust[ym, pl.ds(x, 1), :], TILE),
                    jnp.broadcast_to(crust[ym, pl.ds(x + 1, 1), :], TILE),
                )
                for ym in range(4)
            ]
            for zm in range(4):
                moduli = apart(strided(rows_g, 16 * x + zm, 512))
                place = slab * 16 + 4 * radial + zm
                for ym in range(4):
                    stiff = jnp.where(
                        place >= 16 * slabs - depth[ym], CRUST_FACTOR * moduli[ym], moduli[ym]
                    )
                    at = 4 * zm + ym
                    for side, value in enumerate(twice_events(stiff)):
                        xm = 2 * half + side
                        in_y, in_z = over_y(value, ym), over_z(value, zm)
                        gxj[xm, at] = over_z(in_y, zm) * RHO[xm]
                        gyj[xm, at] = in_z * (RHO[ym] * ASSEMBLED[xm])
                        gzj[xm, at] = in_y * (RHO[zm] * ASSEMBLED[xm])
        for xm in range(4):
            for zm in range(4):
                gy4[j, xm, zm] = next_lane(gyj[xm, 4 * zm])
        wait_load(nat_u, j, 1)
        uj, ubj, uyj = u.at[j], ub.at[0, j], uy.at[j]
        for xm in range(4):
            x = 4 * j + xm
            for zm in range(4):
                values = apart(strided(rows_u, 32 * x + zm, 1024))
                for ym in range(4):
                    uj[xm, 4 * zm + ym] = values[ym]
                    if xm == 0:
                        ubj[4 * zm + ym] = values[ym]
                uyj[xm, zm] = next_lane(values[0])
        for xm in range(4):
            first = pack([gzj[xm, ym] for ym in range(4)], 0)
            ends = [pack([gzj[xm, 4 * zm + ym] for ym in range(4)], 3) for zm in range(4)]
            for zm in range(4):
                kz[j, xm, zm] = ends[zm]
            total = sum(ends[zm] * float(DN[zm, 4] ** 2) for zm in range(4))
            gzs[j, xm] = is0 * total + is1 * first

    def gz_copy(j, count=1):
        at = pl.ds(j, count)
        return pltpu.make_async_remote_copy(
            src_ref=gzs.at[at], dst_ref=gzh.at[at], send_sem=gzsend, recv_sem=gzrecv,
            device_id=other_slab, device_id_type=MESH,
        )

    def z_copy(t, j):
        return pltpu.make_async_remote_copy(
            src_ref=zs.at[t, j], dst_ref=zh.at[t, j], send_sem=zsend, recv_sem=zrecv.at[t, j],
            device_id=other_slab, device_id_type=MESH,
        )

    def u_copy(t):
        return pltpu.make_async_remote_copy(
            src_ref=ub.at[t, 0], dst_ref=ub.at[t, 8], send_sem=usend.at[t], recv_sem=urecv.at[t],
            device_id=before, device_id_type=MESH,
        )

    def g_copy():
        return pltpu.make_async_remote_copy(
            src_ref=gx.at[0, 0], dst_ref=gx.at[8, 0], send_sem=gsend, recv_sem=grecv,
            device_id=before, device_id_type=MESH,
        )

    def p_copy(t):
        return pltpu.make_async_remote_copy(
            src_ref=pb.at[t, 8], dst_ref=pb.at[t, 0], send_sem=psend.at[t], recv_sem=precv.at[t],
            device_id=after, device_id_type=MESH,
        )

    def layer_copy():
        return pltpu.make_async_remote_copy(
            src_ref=layer.at[pl.ds(0, 3)], dst_ref=layer.at[pl.ds(3, 3)], send_sem=qsend, recv_sem=qrecv,
            device_id=after, device_id_type=MESH,
        )

    def h_copy(j):
        at = pl.ds(4 * j, 4)
        return pltpu.make_async_remote_copy(
            src_ref=sent.at[:, at], dst_ref=got.at[:, at], send_sem=hsend.at[j], recv_sem=hrecv.at[j],
            device_id=other_event, device_id_type=MESH,
        )

    @pl.loop(0, 8)
    def _(n):
        j = lax.rem(7 * n, 8)
        set_up(j)

        @pl.when(n == 0)
        def _():
            pl.semaphore_wait(barrier, 4)
            u_copy(0).start()
            g_copy().start()

        gz_copy(j).start()

        @pl.when(n == 1)
        def _():
            for k in range(16):
                g = [gx[7, i, k] for i in range(4)]
                v = [u[7, i, k] for i in range(4)]
                scaled = [g[i] * float(DN[i, 4]) for i in range(4)]
                layer[2, k] = sum(scaled[i] * float(DN[i, 4]) for i in range(4))
                layer[0, k] = sum(
                    scaled[i] * sum(float(DN[i, m]) * v[m] for m in range(4)) for i in range(4)
                )
                layer[1, k] = sum(float(DN[4, m]) * v[m] for m in range(4))
            layer_copy().start()

    def next_coefs(j):
        gj, gn, kj, kn = gx.at[j], gx.at[j + 1, 0], kx.at[j], kdx.at[j + 1]
        for k in range(16):
            scaled = [gj[i, k] * float(DN[i, 4]) for i in range(4)] + [gn[k] * float(DN[4, 4])]
            for m in range(4):
                kj[m, k] = sum(scaled[i] * float(DN[i, m]) for i in range(5))
            kn[k] = sum(scaled[i] * float(DN[i, 4]) for i in range(5))

    def partial_x(t, j):
        uj, kj, pj = u.at[j], kx.at[j], pb.at[t, j + 1]
        for k in range(16):
            pj[k] = (kj[0, k] * uj[0, k] + kj[1, k] * uj[1, k]) + (
                kj[2, k] * uj[2, k] + kj[3, k] * uj[3, k]
            )

    @pl.loop(0, 7)
    def _(j):
        next_coefs(j)
        partial_x(0, j)

    def send_z(t, j):
        uj, zj = u.at[j], zs.at[t, j]

        @pl.when(slab == 0)
        def _():
            kj = kz.at[j]
            for xm in range(4):
                packed = [pack([uj[xm, 4 * zm + ym] for ym in range(4)], 3) for zm in range(4)]
                zj[xm] = (kj[xm, 0] * packed[0] + kj[xm, 1] * packed[1]) + (
                    kj[xm, 2] * packed[2] + kj[xm, 3] * packed[3]
                )

        @pl.when(slab != 0)
        def _():
            for xm in range(4):
                zj[xm] = pack([uj[xm, ym] for ym in range(4)], 0)

        z_copy(t, j).start()

    gz_copy(0, 8).wait_recv()

    @pl.loop(0, 8)
    def _(n):
        j = lax.rem(n + 1, 8)
        gzj, gz4j, kzj, kdzj, gzhj = gz.at[j], gz4.at[j], kz.at[j], kdz.at[j], gzh.at[j]
        for xm in range(4):
            arrived = gzhj[xm]
            above, below = arrived * is0, arrived * is1
            for ym in range(4):
                own = gzj[xm, ym]
                gz4j[xm, ym] = jnp.where(radial == 3, turn(above, 3 - ym), turn(own, 7))
                diagonal = turn(below, -ym) + is1 * float(DN[4, 4] ** 2) * own
                kdzj[xm, ym] = jnp.where(radial == 0, diagonal, 0.0)
            ends = [kzj[xm, zm] for zm in range(4)] + [arrived]
            scaled = [ends[i] * float(DN[i, 4]) for i in range(5)]
            for m in range(4):
                kzj[xm, m] = sum(scaled[i] * float(DN[i, m]) for i in range(5))
        send_z(0, j)

    def advance(j, t, first):
        z_copy(t - 1, j).wait_recv()
        uj, gxj, gyj, gzj, uyj = u.at[j], gx.at[j], gy.at[j], gz.at[j], uy.at[j]
        gy4j, gz4j, kdzj, zhj = gy4.at[j], gz4.at[j], kdz.at[j], zh.at[t - 1, j]
        imj, sfj, wj, hsj = im.at[j], sf.at[j], w.at[j], hs.at[j]
        if first:
            wait_load(nat_m, j, 2)
            wait_load(nat_s, j, 3)
            wait_load(nat_v, j, 4)

        for xm in range(4):
            x = 4 * j + xm
            if first:
                for zm in range(4):
                    if xm % 2 == 0:
                        masses = apart(strided(rows_m, 16 * x + zm, 512))
                        for ym in range(4):
                            mass = masses[ym] * (TIME_STEP * TIME_STEP)
                            one, two = twice_events(mass)
                            imj[xm, 4 * zm + ym], imj[xm + 1, 4 * zm + ym] = one, two
                    values = apart(strided(rows_v, 32 * x + zm, 1024))
                    for ym in range(4):
                        wj[xm, 4 * zm + ym] = values[ym] * TIME_STEP
                    values = apart(strided(rows_s, 32 * x + zm, 1024))
                    for ym in range(4):
                        sfj[xm, 4 * zm + ym] = values[ym] * imj[xm, 4 * zm + ym]
            v = [[uj[xm, 4 * zm + ym] for ym in range(4)] for zm in range(4)]
            f = [[None] * 4 for _ in range(4)]
            arrived = zhj[xm]
            above, below = arrived * is0, arrived * is1
            for ym in range(4):
                u4 = jnp.where(radial == 3, turn(above, 3 - ym), turn(v[0][ym], 7))
                parts = line(
                    *[v[zm][ym] for zm in range(4)], u4,
                    *[gzj[xm, 4 * zm + ym] for zm in range(4)], gz4j[xm, ym],
                )
                carried = jnp.where(radial == 0, turn(below, -ym), turn(parts[4], 1))
                f[0][ym] = (parts[0] + carried) + kdzj[xm, ym] * v[0][ym]
                f[1][ym], f[3][ym] = parts[1], parts[3]
                f[2][ym] = -parts[2]
            for zm in range(4):
                parts = line(
                    *v[zm], uyj[xm, zm], *[gyj[xm, 4 * zm + ym] for ym in range(4)], gy4j[xm, zm]
                )
                fy[xm, zm] = lane_before(parts[4])
                fs[xm, 4 * zm] = f[zm][0] + parts[0]
                fs[xm, 4 * zm + 1] = f[zm][1] + parts[1]
                fs[xm, 4 * zm + 2] = f[zm][2] - parts[2]
                fs[xm, 4 * zm + 3] = f[zm][3] + parts[3]

        strength = jnp.where(upper, time_ref[0, t - 1], time_ref[1, t - 1])
        ubn, pbj, kdxj, gxn = ub.at[t - 1, j + 1], pb.at[t - 1, j], kdx.at[j], gx.at[j + 1, 0]
        for k in range(16):
            v = [uj[i, k] for i in range(4)]
            parts = line(*v, ubn[k], *[gxj[i, k] for i in range(4)], gxn[k], last=False)
            f = [
                fs[0, k] + (parts[0] + (pbj[k] + kdxj[k] * v[0])),
                fs[1, k] + parts[1],
                fs[2, k] - parts[2],
                fs[3, k] + parts[3],
            ]
            for i in range(4):
                if k % 4 == 0:
                    f[i] = f[i] + fy[i, k // 4]
                kick = strength * sfj[i, k] - imj[i, k] * f[i]
                speed = wj[i, k] + kick
                wj[i, k] = speed
                moved = v[i] + speed
                uj[i, k] = moved
                hsj[i, k] = kick * kick if first else hsj[i, k] + kick * kick
                if k % 4 == 0:
                    uyj[i, k // 4] = next_lane(moved)

    def hand_on(j, t):
        send_z(t, j)
        uj, ubj = u.at[j], ub.at[t, j]
        for k in range(16):
            ubj[k] = uj[0, k]
        partial_x(t, j)

        @pl.when(j == 0)
        def _():
            u_copy(t).start()

        @pl.when(j == 7)
        def _():
            p_copy(t).start()

    def end_copy(j, k, e):
        at = pl.ds(4 * j, 4)
        return pltpu.make_async_copy(
            nat_u.at[k, at, e], end_ref.at[e, at, :, pl.ds(128 * k, 128)], end_sem
        )

    def finish(j):
        uj, hsj = u.at[j], hs.at[j]
        for half in range(2):
            for zm in range(4):
                both = []
                for ym in range(4):
                    one, two = hsj[2 * half, 4 * zm + ym], hsj[2 * half + 1, 4 * zm + ym]
                    one = one + pltpu.roll(one, 4, 0)
                    two = two + pltpu.roll(two, 4, 0)
                    both.append(jnp.where(upper, one, two) * (100.0 / (4 * STEPS)))
                for k, value in enumerate(together(both)):
                    first = 512 * k + 16 * (4 * j + 2 * half) + zm
                    rows_sent[pl.ds(first, 8, stride=4), :] = value
        h_copy(j).start()
        for xm in range(4):
            for zm in range(4):
                whole = together([uj[xm, 4 * zm + ym] for ym in range(4)])
                for k, value in enumerate(whole):
                    rows_u[pl.ds(1024 * k + 32 * (4 * j + xm) + zm, 8, stride=4), :] = value
        for k in range(4):
            for e in range(2):
                end_copy(j, k, e).start()

    @pl.loop(0, 8)
    def _(n):
        j = lax.rem(n + 1, 7) + 6 * (n // 7)

        @pl.when(n == 6)
        def _():
            layer_copy().wait_recv()
            for k in range(16):
                own = gx[0, 0, k] * float(DN[4, 4])
                pb[0, 0, k] = layer[3, k] + own * layer[4, k]
                kdx[0, k] = layer[5, k] + own * float(DN[4, 4])

        @pl.when(n == 7)
        def _():
            u_copy(0).wait_recv()
            g_copy().wait_recv()
            next_coefs(7)

        advance(j, 1, True)
        hand_on(j, 1)

    def digit(n, digits, bits):
        words = [
            sum(d << (bits * i) for i, d in enumerate(digits[s : s + 8])) for s in (0, 8, 16)
        ]
        word = jnp.where(n < 8, words[0], jnp.where(n < 16, words[1], words[2]))
        return (word >> (bits * (n & 7))) & ((1 << bits) - 1)

    order_j = (2, 3, 4, 5, 3, 4, 1, 6, 2, 5, 3, 4, 0, 7, 1, 6, 2, 5, 0, 7, 1, 6, 0, 7)
    order_t = (2, 2, 2, 2, 3, 3, 2, 2, 3, 3, 4, 4, 2, 2, 3, 3, 4, 4, 3, 3, 4, 4, 4, 4)

    @pl.loop(0, 24)
    def _(n):
        j = digit(n, order_j, 3)
        t = digit(n, order_t, 3)

        @pl.when(j == 0)
        def _():
            p_copy(t - 1).wait_recv()

        @pl.when(j == 7)
        def _():
            u_copy(t - 1).wait_recv()

        advance(j, t, False)

        @pl.when(t < STEPS)
        def _():
            hand_on(j, t)

        @pl.when(t == STEPS)
        def _():
            finish(j)

    @pl.loop(0, 8)
    def _(n):
        s = n // 2
        j = 3 - s + lax.rem(n, 2) * (1 + 2 * s)
        h_copy(j).wait_recv()
        for xm in range(4):
            x = 4 * j + xm
            for k in range(4):
                hessian_ref[x, :, pl.ds(128 * k, 128)] = sent[k, x] + got[k, x]

    u_copy(0).wait_send()
    g_copy().wait_send()
    layer_copy().wait_send()
    gz_copy(0, 8).wait_send()
    for t in range(1, 4):
        u_copy(t).wait_send()
        p_copy(t).wait_send()

    @pl.loop(0, 8)
    def _(j):
        h_copy(j).wait_send()

    pltpu.make_async_copy(zs, zs, zsend).wait()
    pltpu.make_async_copy(nat_u, nat_u, end_sem).wait()


def per_device(slabs, blocks, *arrays):
    anywhere = pl.BlockSpec(memory_space=pl.ANY)
    inside = pl.BlockSpec(memory_space=pltpu.VMEM)

    def tiles(*shape):
        return pltpu.VMEM((*shape, 8, 128), jnp.float32)

    field, natural = tiles(8, 4, 16), pltpu.VMEM((4, 32, 16, 128), jnp.float32)
    natural_events = pltpu.VMEM((4, 32, 2, 16, 128), jnp.float32)
    several = pltpu.SemaphoreType.DMA
    scratch = [
        natural_events, natural_events, natural_events,
        natural, natural, pltpu.VMEM((32, 512), jnp.int32),
        field, field, field, field, field,
        tiles(9, 4, 16), field, field,
        tiles(8, 4, 4), tiles(8, 4, 4), tiles(8, 4, 4),
        tiles(8, 4, 16), tiles(9, 16), tiles(8, 4, 4), tiles(8, 4, 4),
        tiles(4, 9, 16), tiles(4, 9, 16), tiles(4, 16), tiles(4, 4),
        tiles(4, 8, 4), tiles(4, 8, 4), tiles(8, 4), tiles(8, 4),
        tiles(6, 16), pltpu.VMEM((4, 32, 128), jnp.int32),
        natural, natural, pltpu.VMEM((8, 8, 128), jnp.int32),
        several((8, 5)), several, several, several((4, 8)),
        several, several, several, several,
        several((4,)), several((4,)), several((4,)), several((4,)),
        several, several, several((8,)), several((8,)),
    ]
    return pl.pallas_call(
        functools.partial(body, slabs, blocks),
        out_shape=(
            pltpu.VMEM((2, 32, 16, 512), jnp.float32),
            pltpu.VMEM((32, 16, 512), jnp.float32),
        ),
        in_specs=[anywhere] * 3 + [pl.BlockSpec(memory_space=pltpu.SMEM)] + [anywhere] * 3,
        out_specs=(inside, inside),
        scratch_shapes=scratch,
        compiler_params=pltpu.CompilerParams(
            collective_id=0, has_side_effects=True, vmem_limit_bytes=56 << 20
        ),
        name="adjoint_steps",
    )(*arrays)


def solution(mesh):
    in_specs = (
        P("event", "block", "slab", None),
        P("event", "block", "slab", None),
        P("event", "block", "slab", None),
        P("event", None),
        P("block", "slab", None),
        P("block", "slab", None),
        P("block", None),
    )
    out_specs = (P("event", "block", "slab", None), P("block", "slab", None))
    return jax.shard_map(
        functools.partial(per_device, mesh.shape["slab"], mesh.shape["block"]),
        mesh=mesh, in_specs=in_specs, out_specs=out_specs, check_vma=False,
    )
```

profile of v0, /device:TPU:1, one launch (start us, length us, event | category | flops | bytes accessed | tf_op | source)
XLA Modules:
  0.0 62.4 jit_solution(6146894103702595555)
XLA Ops:
  0.6 59.5 %adjoint_steps.1 = (f32[2,32,16,512]{3,2,1,0:T(8,128)S(1)}, f32[32,16,512]{2,1,0:T(8,128)S(1)}) custom-call(f32[2,32,16,512]{3,2,1,0:T(8,128)} %refs_0_.1, f32[2,32,16,512]{3,2,1,0:T(8,128)} %refs_1_.1, f32[2,32,16,512]{3,2,1,0:T(8,128)} %refs_2_.1, f32[2,4]{1,0:T(2,128)} %refs_3_.1, f32[32,16,512]{2,1,0:T(8,128)} %refs_4_.1, f32[32,16,512]{2,1,0:T(8,128)} %refs_5_.1, ...), custom_call_target="tpu_custom_call" | custom-call | tf_op jit(solution)/shard_map/adjoint_steps/pallas_call | solution.py:594
  60.2 1.3 %copy.11 = f32[2,32,16,512]{3,2,1,0:T(8,128)} copy(f32[2,32,16,512]{3,2,1,0:T(8,128)S(1)} %get-tuple-element.2) | data formatting | bytes 4194304
  61.5 1.0 %copy.12 = f32[32,16,512]{2,1,0:T(8,128)} copy(f32[32,16,512]{2,1,0:T(8,128)S(1)} %get-tuple-element.3) | data formatting | bytes 2097152
where the time goes:
time: 62.6 us; the launch traced here: 62.4 us
  Pallas kernels  59.5 us (95%)
  local copies, waits for them, and re-layouts  2.29 us (4%)
  between operations  0.64 us (1%)
    pallas_call x1, Pallas kernels, per_device(): pl.pallas_call(functools.partial(body, slabs, blocks), out_shape=(pltpu.V...  59.5 us
    unnamed x2, local copies, waits for them, and re-layouts  2.29 us

commit v1 on v0

--- a/solution.py
+++ b/solution.py
@@ -68,6 +68,36 @@
     return fe - fa, ff - fb, total + total, ff + fb, (fe + fa if last else None)
 
 
+ORDER = (
+    (4, 1), (3, 1), (2, 1), (1, 1), (7, 1), (2, 2), (0, 1), (6, 1), (5, 1), (3, 2), (4, 2), (1, 2),
+    (2, 3), (0, 2), (1, 3), (7, 2), (3, 3), (2, 4), (5, 2), (6, 2), (4, 3), (3, 4), (6, 3), (0, 3),
+    (5, 3), (1, 4), (7, 3), (5, 4), (4, 4), (6, 4), (0, 4), (7, 4),
+)
+FIRST_ORDER = [j for j, t in ORDER if t == 1]
+LAST_ORDER = [j for j, t in ORDER if t == STEPS]
+
+
+def digit(n, digits, bits):
+    words = [
+        sum(d << (bits * i) for i, d in enumerate(digits[s : s + 7])) for s in range(0, len(digits), 7)
+    ]
+    word, place = words[0], n
+    for i in range(1, len(words)):
+        word = jnp.where(n < 7 * i, word, words[i])
+        place = jnp.where(n < 7 * i, place, n - 7 * i)
+    return (word >> (bits * place)) & ((1 << bits) - 1)
+
+
+def place_out(end_in, hessian_in, end_out, hessian_out, sem):
+    pairs = [(end_in.at[e, pl.ds(16 * h, 16)], end_out.at[e, pl.ds(16 * h, 16)]) for e in range(2) for h in range(2)]
+    pairs += [(hessian_in.at[pl.ds(16 * h, 16)], hessian_out.at[pl.ds(16 * h, 16)]) for h in range(2)]
+    copies = [pltpu.make_async_copy(*pair, sem.at[i]) for i, pair in enumerate(pairs)]
+    for copy in copies:
+        copy.start()
+    for copy in copies:
+        copy.wait()
+
+
 def body(slabs, blocks, *refs):
     (
         start_hbm, velocity_hbm, source_hbm, time_ref, modulus_hbm, mass_hbm, crust_hbm,
@@ -90,17 +120,19 @@
     for device in (before, after, other_slab, other_event):
         pl.semaphore_signal(barrier, inc=1, device_id=device, device_id_type=MESH)
 
-    def start_loads(j):
+    def start_loads(j, late):
         at = pl.ds(4 * j, 4)
         for k in range(4):
             lanes = (slice(None), pl.ds(128 * k, 128))
-            pairs = [(modulus_hbm.at[at, *lanes], nat_g.at[k, at], 0)]
-            for e in range(2):
-                pairs.append((start_hbm.at[e, at, *lanes], nat_u.at[k, at, e], 1))
-            pairs.append((mass_hbm.at[at, *lanes], nat_m.at[k, at], 2))
-            for e in range(2):
-                pairs.append((source_hbm.at[e, at, *lanes], nat_s.at[k, at, e], 3))
-                pairs.append((velocity_hbm.at[e, at, *lanes], nat_v.at[k, at, e], 4))
+            if late:
+                pairs = [(mass_hbm.at[at, *lanes], nat_m.at[k, at], 2)]
+                for e in range(2):
+                    pairs.append((source_hbm.at[e, at, *lanes], nat_s.at[k, at, e], 3))
+                    pairs.append((velocity_hbm.at[e, at, *lanes], nat_v.at[k, at, e], 4))
+            else:
+                pairs = [(modulus_hbm.at[at, *lanes], nat_g.at[k, at], 0)]
+                for e in range(2):
+                    pairs.append((start_hbm.at[e, at, *lanes], nat_u.at[k, at, e], 1))
             for source, target, kind in pairs:
                 pltpu.make_async_copy(source, target, in_sem.at[j, kind]).start()
 
@@ -113,7 +145,11 @@
 
     @pl.loop(0, 8)
     def _(n):
-        start_loads(lax.rem(7 * n, 8))
+        start_loads(lax.rem(7 * n, 8), False)
+
+    @pl.loop(0, 8)
+    def _(n):
+        start_loads(digit(n, FIRST_ORDER, 4), True)
 
     lane = lax.broadcasted_iota(jnp.int32, TILE, 1)
     row = lax.broadcasted_iota(jnp.int32, TILE, 0)
@@ -485,64 +521,53 @@
             for e in range(2):
                 end_copy(j, k, e).start()
 
+    @pl.loop(0, len(ORDER))
+    def _(n):
+        j = digit(n, [j for j, _ in ORDER], 4)
+        t = digit(n, [t for _, t in ORDER], 4)
+
+        @pl.when(t == 1)
+        def _():
+            @pl.when(j == 0)
+            def _():
+                layer_copy().wait_recv()
+                for k in range(16):
+                    own = gx[0, 0, k] * float(DN[4, 4])
+                    pb[0, 0, k] = layer[3, k] + own * layer[4, k]
+                    kdx[0, k] = layer[5, k] + own * float(DN[4, 4])
+
+            @pl.when(j == 7)
+            def _():
+                u_copy(0).wait_recv()
+                g_copy().wait_recv()
+                next_coefs(7)
+
+            advance(j, t, True)
+            hand_on(j, t)
+
+        @pl.when(t > 1)
+        def _():
+            @pl.when(j == 0)
+            def _():
+                p_copy(t - 1).wait_recv()
+
+            @pl.when(j == 7)
+            def _():
+                u_copy(t - 1).wait_recv()
+
+            advance(j, t, False)
+
+            @pl.when(t < STEPS)
+            def _():
+                hand_on(j, t)
+
+            @pl.when(t == STEPS)
+            def _():
+                finish(j)
+
     @pl.loop(0, 8)
     def _(n):
-        j = lax.rem(n + 1, 7) + 6 * (n // 7)
-
-        @pl.when(n == 6)
-        def _():
-            layer_copy().wait_recv()
-            for k in range(16):
-                own = gx[0, 0, k] * float(DN[4, 4])
-                pb[0, 0, k] = layer[3, k] + own * layer[4, k]
-                kdx[0, k] = layer[5, k] + own * float(DN[4, 4])
-
-        @pl.when(n == 7)
-        def _():
-            u_copy(0).wait_recv()
-            g_copy().wait_recv()
-            next_coefs(7)
-
-        advance(j, 1, True)
-        hand_on(j, 1)
-
-    def digit(n, digits, bits):
-        words = [
-            sum(d << (bits * i) for i, d in enumerate(digits[s : s + 8])) for s in (0, 8, 16)
-        ]
-        word = jnp.where(n < 8, words[0], jnp.where(n < 16, words[1], words[2]))
-        return (word >> (bits * (n & 7))) & ((1 << bits) - 1)
-
-    order_j = (2, 3, 4, 5, 3, 4, 1, 6, 2, 5, 3, 4, 0, 7, 1, 6, 2, 5, 0, 7, 1, 6, 0, 7)
-    order_t = (2, 2, 2, 2, 3, 3, 2, 2, 3, 3, 4, 4, 2, 2, 3, 3, 4, 4, 3, 3, 4, 4, 4, 4)
-
-    @pl.loop(0, 24)
-    def _(n):
-        j = digit(n, order_j, 3)
-        t = digit(n, order_t, 3)
-
-        @pl.when(j == 0)
-        def _():
-            p_copy(t - 1).wait_recv()
-
-        @pl.when(j == 7)
-        def _():
-            u_copy(t - 1).wait_recv()
-
-        advance(j, t, False)
-
-        @pl.when(t < STEPS)
-        def _():
-            hand_on(j, t)
-
-        @pl.when(t == STEPS)
-        def _():
-            finish(j)
-
-    @pl.loop(0, 8)
-    def _(n):
-        s = n // 2
-        j = 3 - s + lax.rem(n, 2) * (1 + 2 * s)
+        j = digit(n, LAST_ORDER, 4)
         h_copy(j).wait_recv()
         for xm in range(4):
             x = 4 * j + xm
@@ -591,7 +616,7 @@
         several((4,)), several((4,)), several((4,)), several((4,)),
         several, several, several((8,)), several((8,)),
     ]
-    return pl.pallas_call(
+    results = pl.pallas_call(
         functools.partial(body, slabs, blocks),
         out_shape=(
             pltpu.VMEM((2, 32, 16, 512), jnp.float32),
@@ -605,6 +630,17 @@
         ),
         name="adjoint_steps",
     )(*arrays)
+    return pl.pallas_call(
+        place_out,
+        out_shape=(
+            jax.ShapeDtypeStruct((2, 32, 16, 512), jnp.float32),
+            jax.ShapeDtypeStruct((32, 16, 512), jnp.float32),
+        ),
+        in_specs=[anywhere] * 2,
+        out_specs=(anywhere, anywhere),
+        scratch_shapes=[several((6,))],
+        name="place_out",
+    )(*results)
 
 
 def solution(mesh):

time: 62.6 us -> 156 us (2.49)
  the two profiles are of different devices: /device:TPU:1 before, /device:TPU:0 now
where the time goes in v1:
time: 156 us
  Pallas kernels  153 us (98%)
  local copies, waits for them, and re-layouts  2.33 us (1%)
    pallas_call x1, Pallas kernels, per_device(): pl.pallas_call(place_out, out_shape=(jax.ShapeDtypeStruct((2, 32, 16, 512...  96.4 us
    pallas_call x1, Pallas kernels, per_device(): pl.pallas_call(functools.partial(body, slabs, blocks), out_shape=(pltpu.V...  56.7 us

profile of v1, /device:TPU:0, one launch (start us, length us, event | category | flops | bytes accessed | tf_op | source)
XLA Modules:
  0.0 156.1 jit_solution(17788740433208335525)
XLA Ops:
  0.6 56.7 %adjoint_steps.1 = (f32[2,32,16,512]{3,2,1,0:T(8,128)S(1)}, f32[32,16,512]{2,1,0:T(8,128)S(1)}) custom-call(f32[2,32,16,512]{3,2,1,0:T(8,128)} %refs_0_.1, f32[2,32,16,512]{3,2,1,0:T(8,128)} %refs_1_.1, f32[2,32,16,512]{3,2,1,0:T(8,128)} %refs_2_.1, f32[2,4]{1,0:T(2,128)} %refs_3_.1, f32[32,16,512]{2,1,0:T(8,128)} %refs_4_.1, f32[32,16,512]{2,1,0:T(8,128)} %refs_5_.1, ...), custom_call_target="tpu_custom_call" | custom-call | tf_op jit(solution)/shard_map/adjoint_steps/pallas_call | solution.py:619
  57.4 0.0 copy-start
  57.4 1.3 copy-done
  58.7 0.0 copy-start.1
  58.7 1.0 copy-done.1
  59.7 96.4 %place_out.1 = (f32[2,32,16,512]{3,2,1,0:T(8,128)}, f32[32,16,512]{2,1,0:T(8,128)}) custom-call(f32[2,32,16,512]{3,2,1,0:T(8,128)} %copy-done, f32[32,16,512]{2,1,0:T(8,128)} %copy-done.1), custom_call_target="tpu_custom_call" | custom-call | tf_op jit(solution)/shard_map/place_out/pallas_call | solution.py:633
Async XLA Ops:
  57.4 1.3 copy-start
  58.7 1.0 copy-start.1

commit v2 on v1

--- a/solution.py
+++ b/solution.py
@@ -73,8 +73,11 @@
     (2, 3), (0, 2), (1, 3), (7, 2), (3, 3), (2, 4), (5, 2), (6, 2), (4, 3), (3, 4), (6, 3), (0, 3),
     (5, 3), (1, 4), (7, 3), (5, 4), (4, 4), (6, 4), (0, 4), (7, 4),
 )
-FIRST_ORDER = [j for j, t in ORDER if t == 1]
-LAST_ORDER = [j for j, t in ORDER if t == STEPS]
+ORDER_OF_FIRST = (
+    (4, 1), (3, 1), (5, 1), (2, 1), (6, 1), (1, 1), (3, 2), (4, 2), (5, 2), (2, 2), (4, 3), (3, 3),
+    (7, 1), (6, 2), (5, 3), (4, 4), (0, 1), (1, 2), (2, 3), (3, 4), (7, 2), (6, 3), (5, 4), (0, 2),
+    (1, 3), (2, 4), (7, 3), (6, 4), (0, 3), (1, 4), (7, 4), (0, 4),
+)
 
 
 def digit(n, digits, bits):
@@ -88,16 +91,6 @@
     return (word >> (bits * place)) & ((1 << bits) - 1)
 
 
-def place_out(end_in, hessian_in, end_out, hessian_out, sem):
-    pairs = [(end_in.at[e, pl.ds(16 * h, 16)], end_out.at[e, pl.ds(16 * h, 16)]) for e in range(2) for h in range(2)]
-    pairs += [(hessian_in.at[pl.ds(16 * h, 16)], hessian_out.at[pl.ds(16 * h, 16)]) for h in range(2)]
-    copies = [pltpu.make_async_copy(*pair, sem.at[i]) for i, pair in enumerate(pairs)]
-    for copy in copies:
-        copy.start()
-    for copy in copies:
-        copy.wait()
-
-
 def body(slabs, blocks, *refs):
     (
         start_hbm, velocity_hbm, source_hbm, time_ref, modulus_hbm, mass_hbm, crust_hbm,
@@ -106,7 +99,7 @@
         u, w, sf, im, hs, gx, gy, gz, uy, gy4, gz4, kx, kdx, kz, kdz, ub, pb, fs, fy,
         zs, zh, gzs, gzh, layer, crust, sent, got, index,
         in_sem, end_sem, zsend, zrecv, gzsend, gzrecv, gsend, grecv,
-        usend, urecv, psend, precv, qsend, qrecv, hsend, hrecv,
+        usend, urecv, psend, precv, qsend, qrecv, hsend, hrecv, ready,
     ) = refs
     block = lax.axis_index("block")
     slab = lax.axis_index("slab")
@@ -116,40 +109,56 @@
     other_slab = (block, 1 - slab, event)
     other_event = (block, slab, 1 - event)
 
+    plane = 8
+    late = lax.rem(block, plane) == 0
+    last = lax.rem(block, plane) == plane - 1
     barrier = pltpu.get_barrier_semaphore()
-    for device in (before, after, other_slab, other_event):
+    for device in (before, other_slab, other_event):
         pl.semaphore_signal(barrier, inc=1, device_id=device, device_id_type=MESH)
 
-    def start_loads(j, late):
-        at = pl.ds(4 * j, 4)
+    @pl.when(jnp.logical_not(last))
+    def _():
+        pl.semaphore_signal(barrier, inc=1, device_id=after, device_id_type=MESH)
+
+    groups = ((0, 1), (7, 1), (1, 6))
+
+    def start_early(group):
+        first, count = groups[group]
+        at = pl.ds(4 * first, 4 * count)
         for k in range(4):
             lanes = (slice(None), pl.ds(128 * k, 128))
-            if late:
-                pairs = [(mass_hbm.at[at, *lanes], nat_m.at[k, at], 2)]
-                for e in range(2):
-                    pairs.append((source_hbm.at[e, at, *lanes], nat_s.at[k, at, e], 3))
-                    pairs.append((velocity_hbm.at[e, at, *lanes], nat_v.at[k, at, e], 4))
-            else:
-                pairs = [(modulus_hbm.at[at, *lanes], nat_g.at[k, at], 0)]
-                for e in range(2):
-                    pairs.append((start_hbm.at[e, at, *lanes], nat_u.at[k, at, e], 1))
+            pairs = [(modulus_hbm.at[at, *lanes], nat_g.at[k, at], 0)]
+            for e in range(2):
+                pairs.append((start_hbm.at[e, at, *lanes], nat_u.at[k, at, e], 1))
             for source, target, kind in pairs:
-                pltpu.make_async_copy(source, target, in_sem.at[j, kind]).start()
-
-    def wait_load(ref, j, kind):
-        whole = ref.at[:, pl.ds(4 * j, 4)]
-        pltpu.make_async_copy(whole, whole, in_sem.at[j, kind]).wait()
+                pltpu.make_async_copy(source, target, in_sem.at[kind, group]).start()
+
+    def wait_early(group):
+        first, count = groups[group]
+        for kind, ref in enumerate((nat_g, nat_u)):
+            part = ref.at[:, pl.ds(4 * first, 4 * count)]
+            pltpu.make_async_copy(part, part, in_sem.at[kind, group]).wait()
+
+    def start_late():
+        for k in range(4):
+            lanes = (slice(None), slice(None), pl.ds(128 * k, 128))
+            pairs = [(mass_hbm.at[*lanes], nat_m.at[k], 0)]
+            for e in range(2):
+                pairs.append((source_hbm.at[e, *lanes], nat_s.at[k, :, e], 1))
+                pairs.append((velocity_hbm.at[e, *lanes], nat_v.at[k, :, e], 2))
+            for source, target, kind in pairs:
+                pltpu.make_async_copy(source, target, in_sem.at[2, kind]).start()
+
+    def wait_late():
+        for kind, ref in enumerate((nat_m, nat_s, nat_v)):
+            pltpu.make_async_copy(ref, ref, in_sem.at[2, kind]).wait()
 
     crust_load = pltpu.make_async_copy(crust_hbm, nat_c, gsend)
     crust_load.start()
 
-    @pl.loop(0, 8)
-    def _(n):
-        start_loads(lax.rem(7 * n, 8), False)
-
-    @pl.loop(0, 8)
-    def _(n):
-        start_loads(digit(n, FIRST_ORDER, 4), True)
+    for group in range(3):
+        start_early(group)
+    start_late()
 
     lane = lax.broadcasted_iota(jnp.int32, TILE, 1)
     row = lax.broadcasted_iota(jnp.int32, TILE, 0)
@@ -227,7 +236,6 @@
             crust[k, at, :] = found[k]
 
     def set_up(j):
-        wait_load(nat_g, j, 0)
         gxj, gyj, gzj = gx.at[j], gy.at[j], gz.at[j]
         for half in range(2):
             x = 4 * j + 2 * half
@@ -256,7 +264,6 @@
         for xm in range(4):
             for zm in range(4):
                 gy4[j, xm, zm] = next_lane(gyj[xm, 4 * zm])
-        wait_load(nat_u, j, 1)
         uj, ubj, uyj = u.at[j], ub.at[0, j], uy.at[j]
         for xm in range(4):
             x = 4 * j + xm
@@ -322,13 +329,29 @@
     @pl.loop(0, 8)
     def _(n):
         j = lax.rem(7 * n, 8)
+        for group in range(3):
+
+            @pl.when(n == group)
+            def _():
+                wait_early(group)
+
         set_up(j)
 
         @pl.when(n == 0)
         def _():
-            pl.semaphore_wait(barrier, 4)
-            u_copy(0).start()
-            g_copy().start()
+            @pl.when(late)
+            def _():
+                pl.semaphore_wait(barrier, 3)
+
+            @pl.when(jnp.logical_not(late))
+            def _():
+                pl.semaphore_wait(barrier, 4)
+                u_copy(0).start()
+                g_copy().start()
+
+            @pl.when(last)
+            def _():
+                pl.semaphore_signal(ready, inc=1, device_id=after, device_id_type=MESH)
 
         gz_copy(j).start()
 
@@ -409,10 +432,6 @@
         uj, gxj, gyj, gzj, uyj = u.at[j], gx.at[j], gy.at[j], gz.at[j], uy.at[j]
         gy4j, gz4j, kdzj, zhj = gy4.at[j], gz4.at[j], kdz.at[j], zh.at[t - 1, j]
         imj, sfj, wj, hsj = im.at[j], sf.at[j], w.at[j], hs.at[j]
-        if first:
-            wait_load(nat_m, j, 2)
-            wait_load(nat_s, j, 3)
-            wait_load(nat_v, j, 4)
 
         for xm in range(4):
             x = 4 * j + xm
@@ -521,10 +540,20 @@
             for e in range(2):
                 end_copy(j, k, e).start()
 
+    wait_late()
+
     @pl.loop(0, len(ORDER))
     def _(n):
-        j = digit(n, [j for j, _ in ORDER], 4)
-        t = digit(n, [t for _, t in ORDER], 4)
+        j, t = [
+            jnp.where(block == 0, digit(n, [task[i] for task in ORDER_OF_FIRST], 4), digit(n, [task[i] for task in ORDER], 4))
+            for i in range(2)
+        ]
+
+        @pl.when(jnp.logical_and(late, n == jnp.where(block == 0, 4, 0)))
+        def _():
+            pl.semaphore_wait(ready, 1)
+            u_copy(0).start()
+            g_copy().start()
 
         @pl.when(t == 1)
         def _():
@@ -567,7 +596,9 @@
 
     @pl.loop(0, 8)
     def _(n):
-        j = digit(n, LAST_ORDER, 4)
+        j = jnp.where(
+            block == 0, *[digit(n, [j for j, t in order if t == STEPS], 4) for order in (ORDER_OF_FIRST, ORDER)]
+        )
         h_copy(j).wait_recv()
         for xm in range(4):
             x = 4 * j + xm
@@ -611,12 +642,13 @@
         tiles(4, 8, 4), tiles(4, 8, 4), tiles(8, 4), tiles(8, 4),
         tiles(6, 16), pltpu.VMEM((4, 32, 128), jnp.int32),
         natural, natural, pltpu.VMEM((8, 8, 128), jnp.int32),
-        several((8, 5)), several, several, several((4, 8)),
+        several((3, 3)), several, several, several((4, 8)),
         several, several, several, several,
         several((4,)), several((4,)), several((4,)), several((4,)),
         several, several, several((8,)), several((8,)),
+        pltpu.SemaphoreType.REGULAR,
     ]
-    results = pl.pallas_call(
+    return pl.pallas_call(
         functools.partial(body, slabs, blocks),
         out_shape=(
             pltpu.VMEM((2, 32, 16, 512), jnp.float32),
@@ -630,17 +662,6 @@
         ),
         name="adjoint_steps",
     )(*arrays)
-    return pl.pallas_call(
-        place_out,
-        out_shape=(
-            jax.ShapeDtypeStruct((2, 32, 16, 512), jnp.float32),
-            jax.ShapeDtypeStruct((32, 16, 512), jnp.float32),
-        ),
-        in_specs=[anywhere] * 2,
-        out_specs=(anywhere, anywhere),
-        scratch_shapes=[several((6,))],
-        name="place_out",
-    )(*results)
 
 
 def solution(mesh):

time: 156 us -> 58.9 us (0.38)
  the two profiles are of different devices: /device:TPU:0 before, /device:TPU:124 now
where the time goes in v2:
time: 58.9 us; the launch traced here: 58.8 us
  Pallas kernels  55.8 us (95%)
  local copies, waits for them, and re-layouts  2.29 us (4%)
  between operations  0.64 us (1%)
    pallas_call x1, Pallas kernels, per_device(): pl.pallas_call(functools.partial(body, slabs, blocks), out_shape=(pltpu.V...  55.8 us
    unnamed x2, local copies, waits for them, and re-layouts  2.29 us

profile of v2, /device:TPU:124, one launch (start us, length us, event | category | flops | bytes accessed | tf_op | source)
XLA Modules:
  0.0 58.8 jit_solution(12654656804107251300)
XLA Ops:
  0.6 55.8 %adjoint_steps.1 = (f32[2,32,16,512]{3,2,1,0:T(8,128)S(1)}, f32[32,16,512]{2,1,0:T(8,128)S(1)}) custom-call(f32[2,32,16,512]{3,2,1,0:T(8,128)} %refs_0_.1, f32[2,32,16,512]{3,2,1,0:T(8,128)} %refs_1_.1, f32[2,32,16,512]{3,2,1,0:T(8,128)} %refs_2_.1, f32[2,4]{1,0:T(2,128)} %refs_3_.1, f32[32,16,512]{2,1,0:T(8,128)} %refs_4_.1, f32[32,16,512]{2,1,0:T(8,128)} %refs_5_.1, ...), custom_call_target="tpu_custom_call" | custom-call | tf_op jit(solution)/shard_map/adjoint_steps/pallas_call | solution.py:651
  56.5 1.3 %copy.11 = f32[2,32,16,512]{3,2,1,0:T(8,128)} copy(f32[2,32,16,512]{3,2,1,0:T(8,128)S(1)} %get-tuple-element.2) | data formatting | bytes 4194304
  57.8 1.0 %copy.12 = f32[32,16,512]{2,1,0:T(8,128)} copy(f32[32,16,512]{2,1,0:T(8,128)S(1)} %get-tuple-element.3) | data formatting | bytes 2097152

commit v3 on v2

--- a/solution.py
+++ b/solution.py
@@ -238,6 +238,20 @@
     def set_up(j):
         gxj, gyj, gzj = gx.at[j], gy.at[j], gz.at[j]
         for half in range(2):
+            for zm in range(4):
+                moduli = apart(strided(rows_g, 16 * (4 * j + 2 * half) + zm, 512))
+                for ym in range(4):
+                    fs[half, 4 * zm + ym] = moduli[ym]
+        uj, ubj, uyj = u.at[j], ub.at[0, j], uy.at[j]
+        for xm in range(4):
+            x = 4 * j + xm
+            for zm in range(4):
+                values = apart(strided(rows_u, 32 * x + zm, 1024))
+                for ym in range(4):
+                    uj[xm, 4 * zm + ym] = values[ym]
+                    if xm == 0:
+                        ubj[4 * zm + ym] = values[ym]
+        for half in range(2):
             x = 4 * j + 2 * half
             depth = [
                 jnp.where(
@@ -248,7 +262,7 @@
                 for ym in range(4)
             ]
             for zm in range(4):
-                moduli = apart(strided(rows_g, 16 * x + zm, 512))
+                moduli = [fs[half, 4 * zm + ym] for ym in range(4)]
                 place = slab * 16 + 4 * radial + zm
                 for ym in range(4):
                     stiff = jnp.where(
@@ -261,19 +275,13 @@
                         gxj[xm, at] = over_z(in_y, zm) * RHO[xm]
                         gyj[xm, at] = in_z * (RHO[ym] * ASSEMBLED[xm])
                         gzj[xm, at] = in_y * (RHO[zm] * ASSEMBLED[xm])
-        for xm in range(4):
-            for zm in range(4):
-                gy4[j, xm, zm] = next_lane(gyj[xm, 4 * zm])
-        uj, ubj, uyj = u.at[j], ub.at[0, j], uy.at[j]
-        for xm in range(4):
-            x = 4 * j + xm
-            for zm in range(4):
-                values = apart(strided(rows_u, 32 * x + zm, 1024))
-                for ym in range(4):
-                    uj[xm, 4 * zm + ym] = values[ym]
-                    if xm == 0:
-                        ubj[4 * zm + ym] = values[ym]
-                uyj[xm, zm] = next_lane(values[0])
+        for half in range(2):
+            for zm in range(4):
+                gy4[j, 2 * half, zm] = next_lane(gyj[2 * half, 4 * zm])
+                gy4[j, 2 * half + 1, zm] = next_lane(gyj[2 * half + 1, 4 * zm])
+        for xm in range(4):
+            for zm in range(4):
+                uyj[xm, zm] = next_lane(uj[xm, 4 * zm])
         for xm in range(4):
             first = pack([gzj[xm, ym] for ym in range(4)], 0)
             ends = [pack([gzj[xm, 4 * zm + ym] for ym in range(4)], 3) for zm in range(4)]
@@ -467,11 +475,15 @@
                 parts = line(
                     *v[zm], uyj[xm, zm], *[gyj[xm, 4 * zm + ym] for ym in range(4)], gy4j[xm, zm]
                 )
-                fy[xm, zm] = lane_before(parts[4])
+                fy[xm, zm] = parts[4]
                 fs[xm, 4 * zm] = f[zm][0] + parts[0]
                 fs[xm, 4 * zm + 1] = f[zm][1] + parts[1]
                 fs[xm, 4 * zm + 2] = f[zm][2] - parts[2]
                 fs[xm, 4 * zm + 3] = f[zm][3] + parts[3]
+
+        for xm in range(4):
+            for zm in range(4):
+                fy[xm, zm] = lane_before(fy[xm, zm])
 
         strength = jnp.where(upper, time_ref[0, t - 1], time_ref[1, t - 1])
         ubn, pbj, kdxj, gxn = ub.at[t - 1, j + 1], pb.at[t - 1, j], kdx.at[j], gx.at[j + 1, 0]
@@ -521,12 +533,14 @@
         uj, hsj = u.at[j], hs.at[j]
         for half in range(2):
             for zm in range(4):
-                both = []
                 for ym in range(4):
                     one, two = hsj[2 * half, 4 * zm + ym], hsj[2 * half + 1, 4 * zm + ym]
                     one = one + pltpu.roll(one, 4, 0)
                     two = two + pltpu.roll(two, 4, 0)
-                    both.append(jnp.where(upper, one, two) * (100.0 / (4 * STEPS)))
+                    fs[half, 4 * zm + ym] = jnp.where(upper, one, two) * (100.0 / (4 * STEPS))
+        for half in range(2):
+            for zm in range(4):
+                both = [fs[half, 4 * zm + ym] for ym in range(4)]
                 for k, value in enumerate(together(both)):
                     first = 512 * k + 16 * (4 * j + 2 * half) + zm
                     rows_sent[pl.ds(first, 8, stride=4), :] = value

time: 58.9 us -> 56.8 us (0.964)
  Pallas kernels: 55.8 us -> 53.7 us
    pallas_call x1, Pallas kernels: 55.8 us -> 53.7 us  [per_device(): pl.pallas_call(functools.partial(body, slabs, blocks), out_shape=(pltpu.V...]
where the time goes in v3:
time: 56.8 us; the launch traced here: 56.7 us
  Pallas kernels  53.7 us (95%)
  local copies, waits for them, and re-layouts  2.29 us (4%)
  between operations  0.64 us (1%)
    pallas_call x1, Pallas kernels, per_device(): pl.pallas_call(functools.partial(body, slabs, blocks), out_shape=(pltpu.V...  53.7 us
    unnamed x2, local copies, waits for them, and re-layouts  2.29 us

profile of v3, /device:TPU:124, one launch (start us, length us, event | category | flops | bytes accessed | tf_op | source)
XLA Modules:
  0.0 56.7 jit_solution(17713431916553954660)
XLA Ops:
  0.6 53.7 %adjoint_steps.1 = (f32[2,32,16,512]{3,2,1,0:T(8,128)S(1)}, f32[32,16,512]{2,1,0:T(8,128)S(1)}) custom-call(f32[2,32,16,512]{3,2,1,0:T(8,128)} %refs_0_.1, f32[2,32,16,512]{3,2,1,0:T(8,128)} %refs_1_.1, f32[2,32,16,512]{3,2,1,0:T(8,128)} %refs_2_.1, f32[2,4]{1,0:T(2,128)} %refs_3_.1, f32[32,16,512]{2,1,0:T(8,128)} %refs_4_.1, f32[32,16,512]{2,1,0:T(8,128)} %refs_5_.1, ...), custom_call_target="tpu_custom_call" | custom-call | tf_op jit(solution)/shard_map/adjoint_steps/pallas_call | solution.py:665
  54.4 1.3 %copy.11 = f32[2,32,16,512]{3,2,1,0:T(8,128)} copy(f32[2,32,16,512]{3,2,1,0:T(8,128)S(1)} %get-tuple-element.2) | data formatting | bytes 4194304
  55.7 1.0 %copy.12 = f32[32,16,512]{2,1,0:T(8,128)} copy(f32[32,16,512]{2,1,0:T(8,128)S(1)} %get-tuple-element.3) | data formatting | bytes 2097152

commit v4 on v3

--- a/solution.py
+++ b/solution.py
@@ -89,6 +89,17 @@
         word = jnp.where(n < 7 * i, word, words[i])
         place = jnp.where(n < 7 * i, place, n - 7 * i)
     return (word >> (bits * place)) & ((1 << bits) - 1)
+
+
+def place_out(end_in, hessian_in, end_out, hessian_out, sem):
+    half = [pl.ds(0, 16), pl.ds(16, 16)]
+    pairs = [(end_in.at[e, at], end_out.at[e, at]) for e in range(2) for at in half]
+    pairs += [(hessian_in.at[at], hessian_out.at[at]) for at in half]
+    copies = [pltpu.make_async_copy(*pair, sem.at[i]) for i, pair in enumerate(pairs)]
+    for copy in copies:
+        copy.start()
+    for copy in copies:
+        copy.wait()
 
 
 def body(slabs, blocks, *refs):
@@ -662,7 +673,7 @@
         several, several, several((8,)), several((8,)),
         pltpu.SemaphoreType.REGULAR,
     ]
-    return pl.pallas_call(
+    results = pl.pallas_call(
         functools.partial(body, slabs, blocks),
         out_shape=(
             pltpu.VMEM((2, 32, 16, 512), jnp.float32),
@@ -676,6 +687,17 @@
         ),
         name="adjoint_steps",
     )(*arrays)
+    return pl.pallas_call(
+        place_out,
+        out_shape=(
+            jax.ShapeDtypeStruct((2, 32, 16, 512), jnp.float32),
+            jax.ShapeDtypeStruct((32, 16, 512), jnp.float32),
+        ),
+        in_specs=[anywhere] * 2,
+        out_specs=(anywhere, anywhere),
+        scratch_shapes=[several((6,))],
+        name="place_out",
+    )(*[pltpu.with_memory_space_constraint(result, pltpu.VMEM) for result in results])
 
 
 def solution(mesh):

time: 56.8 us -> 56.2 us (0.989)
  local copies, waits for them, and re-layouts: 2.29 us -> 0 us
  Pallas kernels: 53.7 us -> 55.5 us
    unnamed x2 -> x0, local copies, waits for them, and re-layouts: 2.29 us -> none
    pallas_call x0 -> x1, Pallas kernels: none -> 1.71 us  [per_device(): pl.pallas_call(place_out, out_shape=(jax.ShapeDtypeStruct((2, 32, 16, 512...]
where the time goes in v4:
time: 56.2 us; the launch traced here: 56.1 us
  Pallas kernels  55.5 us (99%)
  between operations  0.64 us (1%)
    pallas_call x1, Pallas kernels, per_device(): pl.pallas_call(functools.partial(body, slabs, blocks), out_shape=(pltpu.V...  53.7 us
    pallas_call x1, Pallas kernels, per_device(): pl.pallas_call(place_out, out_shape=(jax.ShapeDtypeStruct((2, 32, 16, 512...  1.71 us

profile of v4, /device:TPU:124, one launch (start us, length us, event | category | flops | bytes accessed | tf_op | source)
XLA Modules:
  0.0 56.1 jit_solution(6567660396242465309)
XLA Ops:
  0.6 53.7 %adjoint_steps.1 = (f32[2,32,16,512]{3,2,1,0:T(8,128)S(1)}, f32[32,16,512]{2,1,0:T(8,128)S(1)}) custom-call(f32[2,32,16,512]{3,2,1,0:T(8,128)} %refs_0_.1, f32[2,32,16,512]{3,2,1,0:T(8,128)} %refs_1_.1, f32[2,32,16,512]{3,2,1,0:T(8,128)} %refs_2_.1, f32[2,4]{1,0:T(2,128)} %refs_3_.1, f32[32,16,512]{2,1,0:T(8,128)} %refs_4_.1, f32[32,16,512]{2,1,0:T(8,128)} %refs_5_.1, ...), custom_call_target="tpu_custom_call" | custom-call | tf_op jit(solution)/shard_map/adjoint_steps/pallas_call | solution.py:676
  54.4 1.7 %place_out.1 = (f32[2,32,16,512]{3,2,1,0:T(8,128)}, f32[32,16,512]{2,1,0:T(8,128)}) custom-call(f32[2,32,16,512]{3,2,1,0:T(8,128)S(1)} %get-tuple-element.4.end_in, f32[32,16,512]{2,1,0:T(8,128)S(1)} %get-tuple-element.5.hessian_in), custom_call_target="tpu_custom_call" | custom-call | tf_op jit(solution)/shard_map/place_out/pallas_call | solution.py:690
